TPU v7x, 256 devices: a whole 4x4x8 slice. The times are simulated.
256 devices in a mesh: dp: 4 (over y), expert: 64 (over x, z, core).
Axes of the slice: x: 4, y: 4, z: 8, core: 2. Of those that a mesh axis runs over, the one named last changes fastest.
Arguments:
- tokens: bfloat16 [16384, 2048], P(('dp', 'expert')), may hold values from -6 to 6
- cotangent: bfloat16 [16384, 2048], P(('dp', 'expert')), may hold values from -6 to 6
- expert_ids: int32 [16384, 8], P(('dp', 'expert')), may hold values from 0 to 63, all different within a row; in each aligned block of 64 rows (0 to 63, 64 to 127, ...) at most 8 rows name the same one
- combine: float32 [16384, 8], P(('dp', 'expert')), may hold values from 0.05 to 0.6
- slot_table: int32 [64], replicated, may hold values from 0 to 63, each once
- swap_flags: int32 [32], replicated, may hold values 0 or 1
- weights: bfloat16 [64, 2048, 1152], P('expert', 'dp'), may hold values from -0.125 to 0.125
- moments: float32 [2, 64, 2048, 1152], P(None, 'expert', 'dp'), may hold values from -4.5254834 to 102.4, as said below
Outputs:
- layer_out: bfloat16 [16384, 2048], P(('dp', 'expert'))
- token_grad: bfloat16 [16384, 2048], P(('dp', 'expert'))
- update: bfloat16 [64, 2048, 1152], P('expert', 'dp')
Inputs may be any that keep to these rules, and one draw needn't show every extreme that they name: `expert_ids`: in the rows of one device (aligned blocks of 64 tokens), no expert is named by more than 8 routes, a bound that some block reaches; a token's 8 experts differ. `slot_table`: A permutation: each slot holds one expert. moments[1] is positive.
All inputs are finite; a program needn't handle non-finite values.
Results may differ from a plain program's by a relative error of at most 0.0064.
Values may be sent and summed in bfloat16 or wider, within the bound.
A program may use at most 128 MiB of HBM per device.

v0:
```python
import jax
import jax.numpy as jnp
from jax import lax
from jax.sharding import PartitionSpec as P

beta_one = 0.9
beta_two = 0.999
adam_eps = 1e-08


def from_partner(value, axis, bit):
    mask = 2**bit
    pairs = [(source, source ^ mask) for source in range(lax.axis_size(axis))]
    return lax.ppermute(value, axis, pairs)


def silu_parts(gate_pre):
    sigmoid = jax.nn.sigmoid(gate_pre)
    return (gate_pre * sigmoid, sigmoid * (1.0 + gate_pre * (1.0 - sigmoid)))


def route_sum(returned, cell_index, route_weight, tok_count, top_count):
    model_width = returned.shape[2]
    picked = returned.reshape(-1, model_width)[cell_index]
    picked = picked.astype(jnp.float32).reshape(tok_count, top_count, model_width)
    return jnp.sum(picked * route_weight[:, :, None], axis=1).astype(jnp.bfloat16)


def local(tokens, cotangent, expert_ids, combine, slot_table, swap_flags, weights, moments):
    peer_count = lax.axis_size("expert")
    own_index = lax.axis_index("expert")
    tok_count, model_width = tokens.shape
    top_count = expert_ids.shape[1]
    experts = slot_table.shape[0]
    half_count = experts // 2
    capacity = min(tok_count, tok_count * top_count // experts)
    routes = tok_count * top_count
    top_bit = peer_count.bit_length() - 2
    slot_range = jnp.arange(experts, dtype=jnp.int32)
    pair_range = jnp.arange(half_count, dtype=jnp.int32)
    table_flags = jnp.sum(
        jnp.where(slot_table[:, None] % half_count == pair_range[None, :], swap_flags[None, :], 0),
        axis=1,
    )
    swapped_pair = jnp.sum(jnp.where(pair_range == own_index % half_count, swap_flags, 0)) == 1
    moved_weights = from_partner(weights, "expert", top_bit)
    moved_moments = from_partner(moments, "expert", top_bit)
    weights = jnp.where(swapped_pair, moved_weights, weights)
    moments = jnp.where(swapped_pair, moved_moments, moments)
    dest_table = jnp.where(table_flags == 1, (slot_table + half_count) % experts, slot_table)
    flat_ids = expert_ids.reshape(routes)
    dest_slot = jnp.sum(
        jnp.where(flat_ids[:, None] == slot_range[None, :], dest_table[None, :], 0), axis=1
    )
    dest_hot = (dest_slot[:, None] == slot_range[None, :]).astype(jnp.int32)
    earlier = jnp.cumsum(dest_hot, axis=0) - dest_hot
    position = jnp.sum(earlier * dest_hot, axis=1)
    cell_index = dest_slot * capacity + position
    owner_route = (
        jnp.zeros((experts * capacity,), jnp.int32)
        .at[cell_index]
        .set(jnp.arange(1, routes + 1, dtype=jnp.int32))
    )
    filled = owner_route > 0
    route_pos = jnp.maximum(owner_route - 1, 0)
    token_of = route_pos // top_count
    route_scale = jnp.where(
        filled, combine.reshape(routes)[route_pos], jnp.zeros((), combine.dtype)
    )
    x_send = jnp.where(filled[:, None], tokens[token_of], jnp.zeros((), tokens.dtype)).reshape(
        experts, capacity, model_width
    )
    g_send = (
        (cotangent[token_of].astype(jnp.float32) * route_scale[:, None])
        .astype(jnp.bfloat16)
        .reshape(experts, capacity, model_width)
    )
    gathered = lax.all_gather(weights, "dp", axis=1, tiled=True)[0]
    hidden_width = gathered.shape[1] // 3
    weight_in = gathered[:, : 2 * hidden_width]
    weight_out = gathered[:, 2 * hidden_width :]
    slot_rows = experts * capacity
    x_recv = lax.all_to_all(x_send, "expert", split_axis=0, concat_axis=0, tiled=True)
    expert_rows = x_recv.reshape(slot_rows, model_width)
    projected = jnp.dot(expert_rows, weight_in, preferred_element_type=jnp.float32)
    gate_pre = projected[:, :hidden_width]
    up_pre = projected[:, hidden_width:]
    activated, silu_slope = silu_parts(gate_pre)
    hidden = (activated * up_pre).astype(jnp.bfloat16)
    out_rows = lax.dot_general(
        hidden, weight_out, (((1,), (1,)), ((), ())), preferred_element_type=jnp.float32
    )
    out_rows = out_rows.astype(jnp.bfloat16).reshape(experts, capacity, model_width)
    ones_weight = jnp.ones((tok_count, top_count), jnp.float32)
    back_rows = lax.all_to_all(out_rows, "expert", split_axis=0, concat_axis=0, tiled=True)
    layer_out = route_sum(back_rows, cell_index, combine, tok_count, top_count)
    g_recv = lax.all_to_all(g_send, "expert", split_axis=0, concat_axis=0, tiled=True)
    grad_rows = g_recv.reshape(slot_rows, model_width)
    d_hidden = jnp.dot(grad_rows, weight_out, preferred_element_type=jnp.float32)
    d_pre = jnp.concatenate([d_hidden * up_pre * silu_slope, d_hidden * activated], axis=1).astype(
        jnp.bfloat16
    )
    dx_rows = lax.dot_general(
        d_pre, weight_in, (((1,), (1,)), ((), ())), preferred_element_type=jnp.float32
    )
    dx_rows = dx_rows.astype(jnp.bfloat16).reshape(experts, capacity, model_width)
    dx_back = lax.all_to_all(dx_rows, "expert", split_axis=0, concat_axis=0, tiled=True)
    token_grad = route_sum(dx_back, cell_index, ones_weight, tok_count, top_count)
    grad_in = lax.dot_general(
        expert_rows, d_pre, (((0,), (0,)), ((), ())), preferred_element_type=jnp.float32
    )
    grad_out = lax.dot_general(
        grad_rows, hidden, (((0,), (0,)), ((), ())), preferred_element_type=jnp.float32
    )
    weight_grad = lax.psum_scatter(
        jnp.concatenate([grad_in, grad_out], axis=1), "dp", scatter_dimension=0, tiled=True
    )
    first_new = beta_one * moments[0, 0] + (1.0 - beta_one) * weight_grad
    second_new = beta_two * moments[1, 0] + (1.0 - beta_two) * weight_grad * weight_grad
    adam_step = (first_new / (jnp.sqrt(second_new) + adam_eps)).astype(jnp.bfloat16)[None]
    return (layer_out, token_grad, adam_step)


def solution(mesh):
    in_specs = (
        P(("dp", "expert"), None),
        P(("dp", "expert"), None),
        P(("dp", "expert"), None),
        P(("dp", "expert"), None),
        P(),
        P(),
        P("expert", "dp", None),
        P(None, "expert", "dp", None),
    )
    out_specs = (P(("dp", "expert"), None), P(("dp", "expert"), None), P("expert", "dp", None))
    return jax.shard_map(local, mesh=mesh, in_specs=in_specs, out_specs=out_specs, check_vma=False)
```

profile of v0, /device:TPU:1, one launch (start us, length us, event | category | flops | bytes accessed | tf_op | source)
XLA Modules:
  0.0 356.7 jit_solution(7407284175929919449)
XLA Ops:
  7.2 3.7 %collective-permute-start = (bf16[1,512,1152]{2,1,0:T(8,128)(2,1)}, bf16[1,512,1152]{2,1,0:T(8,128)(2,1)S(1)}, u32[]{:S(2)}, u32[]{:S(2)}) collective-permute-start(bf16[1,512,1152]{2,1,0:T(8,128)(2,1)} %param.14), channel_id=1, source_target_pairs={{0,32},{1,33},{2,34},{3,35},{4,36},{5,37},{6,38},{7,39},{8,40},{9,... | collective-permute-start | bytes 3538952 | tf_op jit(solution)/shard_map/ppermute | solution.py:14
  18.9 3.5 gather_fusion.3
  27.1 10.9 %all-to-all-start = ((bf16[64,8,2048]{2,1,0:T(8,128)(2,1)}), bf16[64,8,2048]{2,1,0:T(8,128)(2,1)}, u32[]{:S(2)}, u32[]{:S(2)}) async-start(bf16[64,8,2048]{2,1,0:T(8,128)(2,1)} %bitcast_select_fusion), calls=%async_computation | async-start | bytes 4194304 | tf_op jit(solution)/shard_map/all_to_all | solution.py:83
  44.8 44.3 %all-to-all-done = bf16[64,8,2048]{2,1,0:T(8,128)(2,1)} async-done(((bf16[64,8,2048]{2,1,0:T(8,128)(2,1)}), bf16[64,8,2048]{2,1,0:T(8,128)(2,1)}, u32[]{:S(2)}, u32[]{:S(2)}) %all-to-all-start) | async-done | bytes 2097184 | tf_op jit(solution)/shard_map/all_to_all | solution.py:83
  89.1 5.8 %all-to-all-start.2 = ((bf16[64,8,2048]{2,1,0:T(8,128)(2,1)}), bf16[64,8,2048]{2,1,0:T(8,128)(2,1)S(1)}, u32[]{:S(2)}, u32[]{:S(2)}) async-start(bf16[64,8,2048]{2,1,0:T(8,128)(2,1)} %fusion), calls=%async_computation.2 | async-start | bytes 4194304 | tf_op jit(solution)/shard_map/all_to_all | solution.py:97
  95.2 4.0 %all-gather.2.cloned.1.call-done = bf16[1,2048,1152]{2,1,0:T(8,128)(2,1)} async-done(((bf16[1,512,1152]{2,1,0:T(8,128)(2,1)}), bf16[1,2048,1152]{2,1,0:T(8,128)(2,1)}) %all-gather.2.cloned.1.call-update) | async-done | bytes 4718608 | tf_op jit(solution)/shard_map/all_gather | solution.py:78
  99.2 5.5 %fusion.3 = f32[512,768]{1,0:T(8,128)} fusion(bf16[2048,1152]{1,0:T(8,128)(2,1)} %bitcast.75, bf16[64,8,2048]{2,1,0:T(8,128)(2,1)} %all-to-all-done), kind=kOutput, calls=%fused_computation.15 | convolution fusion | flops 1610612736 | bytes 6815744 | tf_op jit(solution)/shard_map/dot_general | solution.py:85
  104.6 41.5 %all-to-all-done.2 = bf16[64,8,2048]{2,1,0:T(8,128)(2,1)S(1)} async-done(((bf16[64,8,2048]{2,1,0:T(8,128)(2,1)}), bf16[64,8,2048]{2,1,0:T(8,128)(2,1)S(1)}, u32[]{:S(2)}, u32[]{:S(2)}) %all-to-all-start.2) | async-done | bytes 2097184 | tf_op jit(solution)/shard_map/all_to_all | solution.py:97
  146.2 3.3 multiply_convert_fusion.1
  149.5 2.6 fusion.17
  152.2 3.5 fusion.21
  155.7 6.6 %pad_maximum_fusion = f32[2048,1152]{0,1:T(8,128)} fusion(f32[2048,384]{0,1:T(8,128)} %fusion.17, f32[2048,768]{0,1:T(8,128)S(1)} %fusion.21), kind=kLoop, calls=%fused_computation.6 | loop fusion | flops 2359296 | bytes 18874368 | tf_op jit(solution)/shard_map/concatenate | solution.py:116
  163.4 5.1 %fusion.6 = bf16[64,8,2048]{2,1,0:T(8,128)(2,1)} fusion(bf16[2048,1152]{1,0:T(8,128)(2,1)} %bitcast.77, bf16[512,384]{1,0:T(8,128)(2,1)S(1)} %copy-done.11, bf16[512,384]{1,0:T(8,128)(2,1)S(1)} %copy-done.9), kind=kOutput, calls=%fused_computation.18 | convolution fusion | flops 1613234176 | bytes 6029312 | tf_op jit(solution)/shard_map/dot_general | solution.py:103
  168.5 5.8 %all-to-all-start.3 = ((bf16[64,8,2048]{2,1,0:T(8,128)(2,1)}), bf16[64,8,2048]{2,1,0:T(8,128)(2,1)S(1)}, u32[]{:S(2)}, u32[]{:S(2)}) async-start(bf16[64,8,2048]{2,1,0:T(8,128)(2,1)} %fusion.6), calls=%async_computation.3 | async-start | bytes 4194304 | tf_op jit(solution)/shard_map/all_to_all | solution.py:107
  174.4 6.1 %copy.32 = f32[2,1,512,1152]{2,3,1,0:T(8,128)} copy(f32[2,1,512,1152]{3,2,1,0:T(8,128)} %param.15) | data formatting | bytes 9437184 | tf_op args[7]
  180.5 3.0 collective-permute-start.1
  183.5 4.1 %fusion.5 = bf16[64,8,2048]{2,1,0:T(8,128)(2,1)} fusion(bf16[512,384]{1,0:T(8,128)(2,1)S(1)} %copy-done.6, bf16[2048,1152]{1,0:T(8,128)(2,1)} %bitcast.78), kind=kOutput, calls=%fused_computation.17 | convolution fusion | flops 806354944 | bytes 4063232 | tf_op jit(solution)/shard_map/dot_general | solution.py:90
  187.5 38.1 %all-to-all-done.3 = bf16[64,8,2048]{2,1,0:T(8,128)(2,1)S(1)} async-done(((bf16[64,8,2048]{2,1,0:T(8,128)(2,1)}), bf16[64,8,2048]{2,1,0:T(8,128)(2,1)S(1)}, u32[]{:S(2)}, u32[]{:S(2)}) %all-to-all-start.3) | async-done | bytes 2097184 | tf_op jit(solution)/shard_map/all_to_all | solution.py:107
  225.6 6.1 %all-to-all-start.1 = ((bf16[64,8,2048]{2,1,0:T(8,128)(2,1)}), bf16[64,8,2048]{2,1,0:T(8,128)(2,1)}, u32[]{:S(2)}, u32[]{:S(2)}) async-start(bf16[64,8,2048]{2,1,0:T(8,128)(2,1)} %fusion.5), calls=%async_computation.1 | async-start | bytes 4194304 | tf_op jit(solution)/shard_map/all_to_all | solution.py:95
  231.7 91.3 %collective-permute-done.1 = f32[2,1,512,1152]{2,3,1,0:T(8,128)} collective-permute-done((f32[2,1,512,1152]{2,3,1,0:T(8,128)}, f32[2,1,512,1152]{2,3,1,0:T(8,128)}, u32[]{:S(2)}, u32[]{:S(2)}) %collective-permute-start.1) | collective-permute-done | bytes 4718624 | tf_op jit(solution)/shard_map/ppermute | solution.py:14
  323.0 5.7 %broadcast_select_fusion = f32[2,1,512,1152]{2,3,1,0:T(8,128)} fusion(f32[2,1,512,1152]{2,3,1,0:T(8,128)} %collective-permute-done.1, f32[2,1,512,1152]{2,3,1,0:T(8,128)} %copy.32, pred[]{:T(512)S(6)} %eq.90), kind=kLoop, calls=%fused_computation.29 | loop fusion | flops 1179648 | bytes 14155777 | tf_op jit(solution)/shard_map/jit(_where)/select_n | solution.py:49
  328.7 3.3 gather_fusion.4
  332.0 7.3 %gather_fusion.1 = bf16[512,2048]{1,0:T(8,128)(2,1)} fusion(bf16[512,2048]{1,0:T(8,128)(2,1)} %bitcast.8, s32[1024]{0:T(1024)S(1)} %pad_clamp_fusion.1), kind=kCustom, calls=%fused_computation.1 | custom fusion | bytes 4196352 | tf_op jit(solution)/shard_map/gather | solution.py:24
  344.0 4.5 %fusion.26 = bf16[1,512,1152]{1,2,0:T(8,128)(2,1)S(1)} fusion(f32[512,1152]{0,1:T(8,128)} %reduce-scatter.2.cloned.1.call-done, f32[2,1,512,1152]{2,3,1,0:T(8,128)} %broadcast_select_fusion), kind=kLoop, calls=%fused_computation.42 | loop fusion | flops 5898240 | bytes 8257536 | tf_op jit(solution)/shard_map/broadcast_in_dim | solution.py:120
  (72 shorter events, 26.3 us)
Async XLA Ops:
  7.2 15.9 %copy-start = (bf16[64,2048]{1,0:T(8,128)(2,1)S(1)}, bf16[64,2048]{1,0:T(8,128)(2,1)}, u32[]{:S(2)}) copy-start(bf16[64,2048]{1,0:T(8,128)(2,1)} %param.8) | copy-start | bytes 786436
  7.2 32.1 %collective-permute-start = (bf16[1,512,1152]{2,1,0:T(8,128)(2,1)}, bf16[1,512,1152]{2,1,0:T(8,128)(2,1)S(1)}, u32[]{:S(2)}, u32[]{:S(2)}) collective-permute-start(bf16[1,512,1152]{2,1,0:T(8,128)(2,1)} %param.14), channel_id=1, source_target_pairs={{0,32},{1,33},{2,34},{3,35},{4,36},{5,37},{6,38},{7,39},{8,40},{9,... | collective-permute-start | bytes 3538952 | tf_op jit(solution)/shard_map/ppermute | solution.py:14
  13.7 1.1 copy-start.12
  27.1 10.9 %copy-start.15 = (s32[32]{0:T(128)S(1)}, s32[32]{0:T(128)}, u32[]{:S(2)}) copy-start(s32[32]{0:T(128)} %param.13) | copy-start | bytes 388
  27.1 12.3 %copy-start.7 = (bf16[1,512,1152]{2,1,0:T(8,128)(2,1)S(1)}, bf16[1,512,1152]{2,1,0:T(8,128)(2,1)}, u32[]{:S(2)}) copy-start(bf16[1,512,1152]{2,1,0:T(8,128)(2,1)} %param.14) | copy-start | bytes 3538948
  27.1 62.0 %all-to-all-start = ((bf16[64,8,2048]{2,1,0:T(8,128)(2,1)}), bf16[64,8,2048]{2,1,0:T(8,128)(2,1)}, u32[]{:S(2)}, u32[]{:S(2)}) async-start(bf16[64,8,2048]{2,1,0:T(8,128)(2,1)} %bitcast_select_fusion), calls=%async_computation | async-start | bytes 4194304 | tf_op jit(solution)/shard_map/all_to_all | solution.py:83
  37.9 61.2 %all-gather.2.cloned.1.call-start = ((), (), s32[]{:S(2)}) async-start(), calls=%async_computation.5 | async-start | bytes 5898240 | tf_op jit(solution)/shard_map/all_gather | solution.py:78
  39.3 1.2 copy-start.14
  39.3 1.3 copy-start.2
  89.1 57.1 %all-to-all-start.2 = ((bf16[64,8,2048]{2,1,0:T(8,128)(2,1)}), bf16[64,8,2048]{2,1,0:T(8,128)(2,1)S(1)}, u32[]{:S(2)}, u32[]{:S(2)}) async-start(bf16[64,8,2048]{2,1,0:T(8,128)(2,1)} %fusion), calls=%async_computation.2 | async-start | bytes 4194304 | tf_op jit(solution)/shard_map/all_to_all | solution.py:97
  94.9 249.1 %reduce-scatter.2.cloned.1.call-start = ((), (), s32[]{:S(2)}) async-start(), calls=%async_computation.6 | async-start | bytes 11796480 | tf_op jit(solution)/shard_map/reduce_scatter | solution.py:115
  149.5 2.7 copy-start.5
  149.5 2.7 copy-start.8
  149.5 2.7 copy-start.10
  162.3 1.0 copy-start.9
  162.3 1.1 copy-start.11
  168.5 57.1 %all-to-all-start.3 = ((bf16[64,8,2048]{2,1,0:T(8,128)(2,1)}), bf16[64,8,2048]{2,1,0:T(8,128)(2,1)S(1)}, u32[]{:S(2)}, u32[]{:S(2)}) async-start(bf16[64,8,2048]{2,1,0:T(8,128)(2,1)} %fusion.6), calls=%async_computation.3 | async-start | bytes 4194304 | tf_op jit(solution)/shard_map/all_to_all | solution.py:107
  174.3 9.1 %copy-start.6 = (bf16[512,384]{1,0:T(8,128)(2,1)S(1)}, bf16[512,384]{1,0:T(8,128)(2,1)}, u32[]{:S(2)}) copy-start(bf16[512,384]{1,0:T(8,128)(2,1)} %copy-done.5) | copy-start | bytes 1179652
  180.5 142.6 %collective-permute-start.1 = (f32[2,1,512,1152]{2,3,1,0:T(8,128)}, f32[2,1,512,1152]{2,3,1,0:T(8,128)}, u32[]{:S(2)}, u32[]{:S(2)}) collective-permute-start(f32[2,1,512,1152]{2,3,1,0:T(8,128)} %copy.32), channel_id=1, source_target_pairs={{0,32},{1,33},{2,34},{3,35},{4,36},{5,37},{6,38},{7,39},{8,40},{9,... | collective-permute-start | bytes 14155784 | tf_op jit(solution)/shard_map/ppermute | solution.py:14
  225.6 106.4 %all-to-all-start.1 = ((bf16[64,8,2048]{2,1,0:T(8,128)(2,1)}), bf16[64,8,2048]{2,1,0:T(8,128)(2,1)}, u32[]{:S(2)}, u32[]{:S(2)}) async-start(bf16[64,8,2048]{2,1,0:T(8,128)(2,1)} %fusion.5), calls=%async_computation.1 | async-start | bytes 4194304 | tf_op jit(solution)/shard_map/all_to_all | solution.py:95
  332.0 7.3 %copy-start.3 = (bf16[512,2048]{1,0:T(8,128)(2,1)S(1)}, bf16[512,2048]{1,0:T(8,128)(2,1)}, u32[]{:S(2)}) copy-start(bf16[512,2048]{1,0:T(8,128)(2,1)} %gather_fusion.4) | copy-start | bytes 6291460
  339.3 2.1 copy-start.4
  339.3 2.1 copy-start.13
  344.0 5.9 %copy-start.1 = (bf16[64,2048]{1,0:T(8,128)(2,1)S(1)}, bf16[64,2048]{1,0:T(8,128)(2,1)}, u32[]{:S(2)}) copy-start(bf16[64,2048]{1,0:T(8,128)(2,1)} %param.8) | copy-start | bytes 786436
Sparse Core Ops, SparseCore 0:
  41.2 57.9 all-gather.1
  162.4 88.2 reduce-scatter.1
where the time goes:
time: 358 us; the launch traced here: 357 us
  waiting for transfers between devices  219 us (61%)
  starting transfers between devices  35.5 us (10%)
  local copies, waits for them, and re-layouts  32.3 us (9%)
  other arithmetic  30.6 us (9%)
  matrix products  24.1 us (7%)
  between operations  15 us (4%)
    ppermute x2, waiting for transfers between devices, from_partner(): return lax.ppermute(value, axis, pairs)  91.3 us
    all_to_all x1, waiting for transfers between devices, local(): lax.all_to_all(x_send, 'expert', split_axis=0, concat_axis=0, tiled=True)  44.3 us
    all_to_all x1, waiting for transfers between devices, local(): lax.all_to_all(g_send, 'expert', split_axis=0, concat_axis=0, tiled=True)  41.5 us
    all_to_all x1, waiting for transfers between devices, local(): lax.all_to_all(dx_rows, 'expert', split_axis=0, concat_axis=0, tiled=True)  38.1 us
    all_to_all x1, starting transfers between devices, local(): lax.all_to_all(x_send, 'expert', split_axis=0, concat_axis=0, tiled=True)  10.9 us
    gather x2, local copies, waits for them, and re-layouts, route_sum(): picked = returned.reshape(-1, model_width)[cell_index]  10.6 us
    unnamed x36, local copies, waits for them, and re-layouts  10.2 us
  transfers between devices with their start and end apart: 8, of which 5 were waited for; matrix products, arithmetic and copies ran while one was open for 18% of the time, Pallas kernels for 0%

commit v1 on v0

v1 whole, which is shorter than its diff:
```python
import functools

import jax
import jax.numpy as jnp
from jax import lax
from jax.experimental import pallas as pl
from jax.experimental.pallas import tpu as pltpu
from jax.sharding import PartitionSpec as P

beta_one = 0.9
beta_two = 0.999
adam_eps = 1e-08
MESH = pl.DeviceIdType.MESH
bf16 = jnp.bfloat16
f32 = jnp.float32

NY, NX, NZ, NC = 4, 4, 8, 2
TOK = 64
D = 2048
HALF = D // 2
ROWS = 512
FF = 384
FF2 = 2 * FF
FF3 = 3 * FF
PART = D // NY
PIECE = PART // 4


def dot(a, b, ca=1, cb=0):
    return lax.dot_general(a, b, (((ca,), (cb,)), ((), ())), preferred_element_type=f32)


def kernel(
    flags, info_ref, tok_ref, cot_ref, w_ref, mom_ref,
    lo_ref, tg_ref, up_ref,
    info_all, pick, back_one, back_hi, back_lo, scale,
    near, xs, xr, wg, orow, orecv, rs_out, rs_in,
    gsend, gown, grecv, mom, uown, urecv, proj, hidden, d_pre,
    local_sem, info_sem, zsend, zrecv, xsend, xrecv, xlocal, wsend, wrecv,
    osend, orecv_sem, olocal, rsend, rrecv, gsend_sem, grecv_sem, usend, urecv_sem,
):
    y = lax.axis_index("dp")
    e = lax.axis_index("expert")
    x = lax.div(e, NZ * NC)
    z = lax.div(lax.rem(e, NZ * NC), NC)
    c = lax.rem(e, NC)
    me = x * NC + c

    def xdev(j):
        return (y, lax.div(j, NC) * (NZ * NC) + z * NC + lax.rem(j, NC))

    def zdev(k):
        return (y, x * (NZ * NC) + k * NC + c)

    def zat(off):
        return lax.rem(z + (off % NZ), NZ)

    def yat(off):
        return lax.rem(y + (off % NY), NY)

    znext = (zdev(zat(1)), zdev(zat(-1)))
    ynext = ((yat(1), e), (yat(-1), e))

    def rcopy(src, dst, ssem, rsem, dev):
        return pltpu.make_async_remote_copy(
            src_ref=src, dst_ref=dst, send_sem=ssem, recv_sem=rsem, device_id=dev, device_id_type=MESH
        )

    def await_bytes(ref, sem):
        pltpu.make_async_copy(ref, ref, sem).wait()

    mom_copy = pltpu.make_async_copy(mom_ref, mom, local_sem.at[0])
    mom_copy.start()
    w_copy = pltpu.make_async_copy(w_ref, wg.at[pl.ds(y * PART, PART)], local_sem.at[1])
    w_copy.start()

    bar = pltpu.get_barrier_semaphore()
    for r in range(1, 8):
        for dev in (xdev(lax.rem(me + r, 8)), zdev(zat(r))):
            pl.semaphore_signal(bar, inc=1, device_id=dev, device_id_type=MESH)
    for dev in ynext:
        pl.semaphore_signal(bar, inc=1, device_id=dev, device_id_type=MESH)
    pl.semaphore_wait(bar, 16)

    for r in range(1, NZ):
        rcopy(info_ref, info_all.at[z], info_sem.at[0], info_sem.at[1], zdev(zat(r))).start()

    def send_own(t):
        src = (tok_ref, cot_ref)[t]
        for h in (0, 1):
            for way in (0, 1):
                rcopy(
                    src.at[:, pl.ds(h * HALF, HALF)], near.at[t, z, h],
                    zsend.at[t, way], zrecv.at[t, way, 0, h], znext[way],
                ).start()

    send_own(0)
    for way in (0, 1):
        for h in (way, 1 - way):
            rows = pl.ds(h * (PART // 2), PART // 2)
            rcopy(
                w_ref.at[rows], wg.at[pl.ds(y * PART + h * (PART // 2), PART // 2)],
                wsend.at[way], wrecv.at[way, h], ynext[way],
            ).start()

    def weights_on():
        for way in (0, 1):
            base = yat(-1 if way == 0 else 1) * PART + way * (PART // 2)
            rows = wg.at[pl.ds(base, PART // 2)]
            await_bytes(rows, wrecv.at[way, way])
            rcopy(rows, rows, wsend.at[way], wrecv.at[way, 2], ynext[way]).start()

    def weights_in():
        w_copy.wait()
        for way in (0, 1):
            base = yat(-1 if way == 0 else 1) * PART + (1 - way) * (PART // 2)
            await_bytes(wg.at[pl.ds(base, PART // 2)], wrecv.at[way, 1 - way])
            base = yat(2) * PART + way * (PART // 2)
            await_bytes(wg.at[pl.ds(base, PART // 2)], wrecv.at[way, 2])

    info_all[z] = info_ref[...]
    await_bytes(info_all.at[pl.ds(0, NZ - 1)], info_sem.at[1])
    before = (
        lax.broadcasted_iota(jnp.int32, (128, 128), 0) < lax.broadcasted_iota(jnp.int32, (128, 128), 1)
    ).astype(f32)
    j_col = lax.broadcasted_iota(jnp.int32, (8, 128), 0)
    slots = ((j_col // NC) * (NZ * NC) + z * NC + j_col % NC).astype(f32)
    place = lax.broadcasted_iota(jnp.int32, (16, 128), 0)

    def tables(off, carry):
        one = info_all[lax.rem(z + off, NZ)]
        here = jnp.zeros((8, 128), f32)
        weight = jnp.zeros((8, 128), f32)
        for k in range(8):
            same = jnp.broadcast_to(one[k : k + 1], (8, 128)) == slots
            here = here + jnp.where(same, 1.0, 0.0)
            weight = weight + jnp.where(same, jnp.broadcast_to(one[8 + k : 9 + k], (8, 128)), 0.0)
        rank = dot(here, before)
        second = jnp.where((off >= 1) & (off <= 4), 1, 0)
        rank = jnp.where(here > 0.5, rank, 99.0)
        wanted = (place - second * 8).astype(f32)
        wanted = jnp.where((wanted >= 0.0) & (wanted < 8.0), wanted, -1.0)
        hot = []
        heavy = []
        for j in range(8):
            is_it = jnp.broadcast_to(rank[j : j + 1], (16, 128)) == wanted
            hot.append(jnp.where(is_it, 1.0, 0.0))
            heavy.append(jnp.where(is_it, jnp.broadcast_to(weight[j : j + 1], (16, 128)), 0.0))
        hot = jnp.concatenate(hot, axis=0)
        heavy = jnp.concatenate(heavy, axis=0)
        pick[off] = hot.astype(bf16)
        scale[off] = jnp.broadcast_to(jnp.sum(heavy, axis=1, keepdims=True), (128, 128))
        back_one[off] = hot.T.astype(bf16)
        turned = heavy.T
        high = turned.astype(bf16)
        back_hi[off] = high
        back_lo[off] = (turned - high.astype(f32)).astype(bf16)
        return carry

    lax.fori_loop(0, NZ, tables, 0)

    def gather(t, s, h, off_a, off_b, rows_a, rows_b):
        cols = pl.ds(h * HALF, HALF)
        rows = dot(pick[off_a][:, :TOK], rows_a) + dot(pick[off_b][:, :TOK], rows_b)
        if t == 1:
            rows = rows * (scale[off_a][:, :1] + scale[off_b][:, :1])
        xs[t, s, :, cols] = rows.astype(bf16)
        mine = pl.ds(me * 64 + s * 16, 16)

        def send(r, carry):
            j = lax.rem(me + r, 8)
            rcopy(
                xs.at[t, s, pl.ds(j * 16, 16), cols], xr.at[t, mine, cols],
                xsend.at[t], xrecv.at[t], xdev(j),
            ).start()
            return carry

        lax.fori_loop(1, 8, send, 0)
        pltpu.make_async_copy(xs.at[t, s, pl.ds(me * 16, 16), cols], xr.at[t, mine, cols], xlocal.at[t]).start()

    def step(t, s, h):
        for way in (0, 1):
            chunk = near.at[t, zat(-s if way == 0 else s), h]
            await_bytes(chunk, zrecv.at[t, way, s - 1, h])
            if s < 3 or h == way:
                rcopy(chunk, chunk, zsend.at[t, way], zrecv.at[t, way, s, h], znext[way]).start()
        gather(t, s, h, NZ - s, s, near[t, zat(-s), h], near[t, zat(s), h])

    def last_step(t, h):
        far = zat(4)
        await_bytes(near.at[t, far, h], zrecv.at[t, h, 3, h])
        own = (tok_ref, cot_ref)[t][:, h * HALF : (h + 1) * HALF]
        gather(t, 0, h, 0, 4, own, near[t, far, h])

    for s in (1, 2, 3):
        for h in (0, 1):
            step(0, s, h)
        if s == 2:
            send_own(1)
        if s == 3:
            weights_on()
    for h in (0, 1):
        last_step(0, h)
    for s in (1, 2, 3):
        for h in (0, 1):
            step(1, s, h)
    for h in (0, 1):
        last_step(1, h)

    def rows_in(t):
        await_bytes(xr.at[t, pl.ds(0, 448)], xrecv.at[t])
        await_bytes(xr.at[t, pl.ds(0, 64)], xlocal.at[t])

    rows_in(0)
    weights_in()

    def project(n, carry):
        cols = pl.ds(pl.multiple_of(n * 256, 256), 256)
        proj[:, cols] = dot(xr[0], wg[:, cols])
        return carry

    lax.fori_loop(0, 3, project, 0)

    def activate(n, carry):
        rows = pl.ds(pl.multiple_of(n * 64, 64), 64)
        gate = proj[rows, :FF]
        hidden[rows] = (gate * jax.nn.sigmoid(gate) * proj[rows, FF:]).astype(bf16)
        return carry

    lax.fori_loop(0, 8, activate, 0)

    def out_rows(n, carry):
        part = pl.ds(pl.multiple_of(n * 256, 256), 256)
        orow[0, :, part] = dot(hidden[...], wg[part, FF2:], 1, 1).astype(bf16)
        return carry

    lax.fori_loop(0, 8, out_rows, 0)

    def send_back(t):
        for s in (0, 3, 2, 1):
            def send(r, carry, s=s):
                j = lax.rem(me + r, 8)
                rcopy(
                    orow.at[t, pl.ds(j * 64 + s * 16, 16)], orecv.at[t, s, pl.ds(me * 16, 16)],
                    osend.at[t], orecv_sem.at[t, s], xdev(j),
                ).start()
                return carry

            lax.fori_loop(1, 8, send, 0)
            pltpu.make_async_copy(
                orow.at[t, pl.ds(me * 64 + s * 16, 16)], orecv.at[t, s, pl.ds(me * 16, 16)], olocal.at[t, s]
            ).start()

    send_back(0)

    rows_in(1)

    def backward(n, carry):
        rows = pl.ds(pl.multiple_of(n * 256, 256), 256)
        d_hidden = dot(xr[1, rows], wg[:, FF2:])
        gate = proj[rows, :FF]
        up = proj[rows, FF:]
        sig = jax.nn.sigmoid(gate)
        d_pre[rows, :FF] = (d_hidden * up * (sig * (1.0 + gate * (1.0 - sig)))).astype(bf16)
        d_pre[rows, FF:] = (d_hidden * (gate * sig)).astype(bf16)
        return carry

    lax.fori_loop(0, 2, backward, 0)

    def weight_grad(off, dest):
        base = yat(off) * PART

        def half(n, carry):
            cols = pl.ds(pl.multiple_of(base + n * 256, 256), 256)
            rows = pl.ds(pl.multiple_of(n * 256, 256), 256)
            dest[rows, :FF2] = dot(xr[0, :, cols], d_pre[...], 0, 0).astype(dest.dtype)
            dest[rows, FF2:] = dot(xr[1, :, cols], hidden[...], 0, 0).astype(dest.dtype)
            return carry

        lax.fori_loop(0, 2, half, 0)

    def send_grad(way, message, block, piece):
        rcopy(
            gsend.at[block, pl.ds(piece * PIECE, PIECE)], grecv.at[way, message],
            gsend_sem.at[way], grecv_sem.at[way, message], ynext[way],
        ).start()

    weight_grad(2, gsend.at[0])
    send_grad(0, 0, 0, 0)
    send_grad(1, 0, 0, 2)
    weight_grad(1, gsend.at[1])
    send_grad(0, 1, 1, 2)
    weight_grad(-1, gsend.at[2])
    send_grad(1, 1, 2, 0)

    def pass_on(first):
        for way in (0, 1):
            message = 0 if first else 3
            piece = (0 if way == 0 else 2) + (0 if first else 1)
            await_bytes(grecv.at[way, message], grecv_sem.at[way, message])

            def add(n, carry, way=way, message=message, piece=piece):
                there = pl.ds(pl.multiple_of(piece * PIECE + n * 16, 16), 16)
                here = pl.ds(pl.multiple_of(n * 16, 16), 16)
                total = gsend[1 + way, there].astype(f32) + grecv[way, message, here].astype(f32)
                gsend[1 + way, there] = total.astype(bf16)
                return carry

            lax.fori_loop(0, PIECE // 16, add, 0)
            send_grad(way, message + 2, 1 + way, piece)

    def second_round():
        send_grad(0, 3, 0, 1)
        send_grad(1, 3, 0, 3)
        send_grad(0, 4, 1, 3)
        send_grad(1, 4, 2, 1)

    def adam(first):
        for low in (True, False):
            piece = (0 if low else 2) + (0 if first else 1)
            done, plain = (2, 1) if first else (5, 4)
            from_low, from_high = (done, plain) if low else (plain, done)
            await_bytes(grecv.at[0, from_low], grecv_sem.at[0, from_low])
            await_bytes(grecv.at[1, from_high], grecv_sem.at[1, from_high])

            def rows_of(n, carry, piece=piece, from_low=from_low, from_high=from_high):
                there = pl.ds(pl.multiple_of(piece * PIECE + n * 16, 16), 16)
                here = pl.ds(pl.multiple_of(n * 16, 16), 16)
                grad = gown[there] + grecv[0, from_low, here].astype(f32) + grecv[1, from_high, here].astype(f32)
                first_new = beta_one * mom[0, there] + (1.0 - beta_one) * grad
                second_new = beta_two * mom[1, there] + (1.0 - beta_two) * grad * grad
                uown[there] = (first_new / (jnp.sqrt(second_new) + adam_eps)).astype(bf16)
                return carry

            lax.fori_loop(0, PIECE // 16, rows_of, 0)
            rows = pl.ds(piece * PIECE, PIECE)
            rcopy(
                uown.at[rows], urecv.at[rows], usend.at[0], urecv_sem.at[piece],
                xdev(lax.rem(me + 4, 8)),
            ).start()

    def partial(t, off, s, cols):
        rows = orecv[t, s, :, cols]
        if t == 1:
            return dot(back_one[off][:TOK], rows)
        return dot(back_hi[off][:TOK], rows) + dot(back_lo[off][:TOK], rows)

    def over_tiles(h, body):
        def tile(n, carry):
            inner = pl.multiple_of(n * 256, 256)
            body(pl.ds(pl.multiple_of(h * HALF + inner, 256), 256), pl.ds(inner, 256))
            return carry

        lax.fori_loop(0, HALF // 256, tile, 0)

    def reduce_step(t, k):
        s = (4 - k) % 4
        await_bytes(orecv.at[t, s, pl.ds(0, 112)], orecv_sem.at[t, s])
        await_bytes(orecv.at[t, s, pl.ds(0, 16)], olocal.at[t, s])
        for way in (0, 1):
            off = (4 - k) if way == 0 else (4 + k)
            if k == 1:
                await_bytes(rs_in.at[t, way, 0, way], rrecv.at[t, way, 0])
            if k > 1:
                await_bytes(rs_in.at[t, way, k - 1], rrecv.at[t, way, k - 1])
            for h in (0, 1):
                if k == 0 and h != way:
                    continue

                def one(cols, inner, way=way, off=off, h=h):
                    total = partial(t, off, s, cols)
                    if k > 1 or (k == 1 and h == way):
                        total = total + rs_in[t, way, k - 1, h, :, inner].astype(f32)
                    rs_out[t, way, k, h, :, inner] = total.astype(bf16)

                over_tiles(h, one)
            out, into = rs_out.at[t, way, k], rs_in.at[t, way, k]
            if k == 0:
                out, into = out.at[way], into.at[way]
            rcopy(out, into, rsend.at[t, way, k], rrecv.at[t, way, k], znext[way]).start()

    def reduce_last(t):
        for way in (0, 1):
            await_bytes(rs_in.at[t, way, 3], rrecv.at[t, way, 3])
        for h in (0, 1):
            def one(cols, inner, h=h):
                total = partial(t, 0, 0, cols)
                total = total + rs_in[t, 0, 3, h, :, inner].astype(f32) + rs_in[t, 1, 3, h, :, inner].astype(f32)
                (lo_ref, tg_ref)[t][:, cols] = total.astype(bf16)

            over_tiles(h, one)

    reduce_step(0, 0)

    def dx_rows(n, carry):
        part = pl.ds(pl.multiple_of(n * 256, 256), 256)
        orow[1, :, part] = dot(d_pre[...], wg[part, :FF2], 1, 1).astype(bf16)
        return carry

    lax.fori_loop(0, 8, dx_rows, 0)
    send_back(1)
    pass_on(True)
    second_round()
    reduce_step(0, 1)
    weight_grad(0, gown)
    mom_copy.wait()
    reduce_step(0, 2)
    reduce_step(0, 3)
    adam(True)
    reduce_step(1, 0)
    reduce_last(0)
    pass_on(False)
    reduce_step(1, 1)
    reduce_step(1, 2)
    adam(False)
    reduce_step(1, 3)
    reduce_last(1)

    swapped = jnp.full((16, FF3), flags[lax.rem(e, NX * NZ * NC // 2)], jnp.int32) == 1
    for piece in (0, 2, 1, 3):
        await_bytes(urecv.at[pl.ds(piece * PIECE, PIECE)], urecv_sem.at[piece])

        def choose(n, carry, piece=piece):
            there = pl.ds(pl.multiple_of(piece * PIECE + n * 16, 16), 16)
            up_ref[there] = jnp.where(swapped, urecv[there].astype(f32), uown[there].astype(f32)).astype(bf16)
            return carry

        lax.fori_loop(0, PIECE // 16, choose, 0)

    await_bytes(info_all.at[pl.ds(0, NZ - 1)], info_sem.at[0])
    await_bytes(uown, usend.at[0])
    for way in (0, 1):
        await_bytes(wg.at[pl.ds(0, PART + PART // 2)], wsend.at[way])
        await_bytes(grecv.at[way], gsend_sem.at[way])
    for t in (0, 1):
        await_bytes(xr.at[t, pl.ds(0, 448)], xsend.at[t])
        await_bytes(orow.at[t, pl.ds(0, 448)], osend.at[t])
        for way in (0, 1):
            await_bytes(near.at[t, pl.ds(0, 7), 0], zsend.at[t, way])
            await_bytes(rs_out.at[t, way, 0, way], rsend.at[t, way, 0])
            for k in (1, 2, 3):
                await_bytes(rs_out.at[t, way, k], rsend.at[t, way, k])


def local(tokens, cotangent, expert_ids, combine, slot_table, swap_flags, weights, moments):
    experts = slot_table.shape[0]
    slot_range = jnp.arange(experts, dtype=jnp.int32)
    turned = expert_ids.T
    slots = jnp.sum(
        jnp.where(turned[:, :, None] == slot_range[None, None, :], slot_table[None, None, :], 0), axis=2
    )
    info = jnp.concatenate([slots.astype(f32), combine.T], axis=0)
    info = jnp.pad(info, ((0, 0), (0, 128 - TOK)), constant_values=-1.0)
    vmem = pl.BlockSpec(memory_space=pltpu.VMEM)
    anyw = pl.BlockSpec(memory_space=pl.ANY)
    dma = pltpu.SemaphoreType.DMA
    layer_out, token_grad, update = pl.pallas_call(
        kernel,
        out_shape=(
            jax.ShapeDtypeStruct((TOK, D), bf16),
            jax.ShapeDtypeStruct((TOK, D), bf16),
            jax.ShapeDtypeStruct((PART, FF3), bf16),
        ),
        in_specs=[pl.BlockSpec(memory_space=pltpu.SMEM), vmem, vmem, vmem, anyw, anyw],
        out_specs=(vmem, vmem, vmem),
        scratch_shapes=[
            pltpu.VMEM((NZ, 16, 128), f32),
            pltpu.VMEM((NZ, 128, 128), bf16),
            pltpu.VMEM((NZ, 128, 128), bf16),
            pltpu.VMEM((NZ, 128, 128), bf16),
            pltpu.VMEM((NZ, 128, 128), bf16),
            pltpu.VMEM((NZ, 128, 128), f32),
            pltpu.VMEM((2, NZ, 2, TOK, HALF), bf16),
            pltpu.VMEM((2, 4, 128, D), bf16),
            pltpu.VMEM((2, ROWS, D), bf16),
            pltpu.VMEM((D, FF3), bf16),
            pltpu.VMEM((2, ROWS, D), bf16),
            pltpu.VMEM((2, 4, 128, D), bf16),
            pltpu.VMEM((2, 2, 4, 2, TOK, HALF), bf16),
            pltpu.VMEM((2, 2, 4, 2, TOK, HALF), bf16),
            pltpu.VMEM((3, PART, FF3), bf16),
            pltpu.VMEM((PART, FF3), f32),
            pltpu.VMEM((2, 6, PIECE, FF3), bf16),
            pltpu.VMEM((2, PART, FF3), f32),
            pltpu.VMEM((PART, FF3), bf16),
            pltpu.VMEM((PART, FF3), bf16),
            pltpu.VMEM((ROWS, FF2), f32),
            pltpu.VMEM((ROWS, FF), bf16),
            pltpu.VMEM((ROWS, FF2), bf16),
            dma((2,)),
            dma((2,)),
            dma((2, 2)),
            dma((2, 2, 4, 2)),
            dma((2,)),
            dma((2,)),
            dma((2,)),
            dma((2,)),
            dma((2, 3)),
            dma((2,)),
            dma((2, 4)),
            dma((2, 4)),
            dma((2, 2, 4)),
            dma((2, 2, 4)),
            dma((2,)),
            dma((2, 6)),
            dma((1,)),
            dma((4,)),
        ],
        compiler_params=pltpu.CompilerParams(
            collective_id=0, has_side_effects=True, vmem_limit_bytes=62 * 2**20
        ),
        cost_estimate=pl.CostEstimate(flops=8 * 10**9, bytes_accessed=9 * 10**6, transcendentals=10**6),
        name="moe_step",
    )(swap_flags, info, tokens, cotangent, weights[0], moments[:, 0])
    return layer_out, token_grad, update[None]


def solution(mesh):
    in_specs = (
        P(("dp", "expert"), None),
        P(("dp", "expert"), None),
        P(("dp", "expert"), None),
        P(("dp", "expert"), None),
        P(),
        P(),
        P("expert", "dp", None),
        P(None, "expert", "dp", None),
    )
    out_specs = (P(("dp", "expert"), None), P(("dp", "expert"), None), P("expert", "dp", None))
    return jax.shard_map(local, mesh=mesh, in_specs=in_specs, out_specs=out_specs, check_vma=False)
```

time: 358 us -> 154 us (0.43)
  the two profiles are of different devices: /device:TPU:1 before, /device:TPU:109 now
where the time goes in v1:
time: 154 us; the launch traced here: 153 us
  Pallas kernels  145 us (94%)
  local copies, waits for them, and re-layouts  5.71 us (4%)
  other arithmetic  2.32 us (2%)
    pallas_call x1, Pallas kernels, local(): pl.pallas_call(kernel, out_shape=(jax.ShapeDtypeStruct((TOK, D), bf16), j...  145 us
    unnamed x3, local copies, waits for them, and re-layouts  5.71 us

profile of v1, /device:TPU:109, one launch (start us, length us, event | category | flops | bytes accessed | tf_op | source)
XLA Modules:
  0.0 153.2 jit_solution(1891393834373959470)
XLA Ops:
  0.6 1.0 select_reduce_fusion
  1.7 1.3 select_maximum_fusion.info_ref
  3.0 144.6 %moe_step.1 = (bf16[64,2048]{1,0:T(8,128)(2,1)}, bf16[64,2048]{1,0:T(8,128)(2,1)}, bf16[512,1152]{1,0:T(8,128)(2,1)}) custom-call(s32[32]{0:T(128)} %flags.1, f32[16,128]{1,0:T(8,128)} %select_maximum_fusion.info_ref, bf16[64,2048]{1,0:T(8,128)(2,1)} %tok_ref.1, bf16[64,2048]{1,0:T(8,128)(2,1)} %cot_ref.1, bf16[512,1152]{1,0:T(8,128)(2,1)} %bitcast.9, ...), custom_call_target="tpu_custom_call" | custom-call | flops 8000000000 | bytes 9000000 | tf_op jit(solution)/shard_map/moe_step/pallas_call | solution.py:457
  147.5 1.7 %copy.14 = bf16[64,2048]{1,0:T(8,128)(2,1)} copy(bf16[64,2048]{1,0:T(8,128)(2,1)} %get-tuple-element.12) | data formatting | bytes 524288
  149.2 1.7 %copy.15 = bf16[64,2048]{1,0:T(8,128)(2,1)} copy(bf16[64,2048]{1,0:T(8,128)(2,1)} %get-tuple-element.13) | data formatting | bytes 524288
  150.9 2.4 %copy.16 = bf16[1,512,1152]{2,1,0:T(8,128)(2,1)} copy(bf16[1,512,1152]{2,1,0:T(8,128)(2,1)} %bitcast.5) | data formatting | bytes 2359296
  (1 shorter events, 0.0 us)

commit v2 on v1

--- a/solution.py
+++ b/solution.py
@@ -31,12 +31,12 @@
 
 
 def kernel(
-    flags, info_ref, tok_ref, cot_ref, w_ref, mom_ref,
+    flags, table, ids_ref, comb_ref, tok_ref, cot_ref, w_ref, mom_ref,
     lo_ref, tg_ref, up_ref,
-    info_all, pick, back_one, back_hi, back_lo, scale,
+    info_ref, info_all, sums, upd, fold, pick, xs_alone, back_one, back_hi, back_lo, scale,
     near, xs, xr, wg, orow, orecv, rs_out, rs_in,
     gsend, gown, grecv, mom, uown, urecv, proj, hidden, d_pre,
-    local_sem, info_sem, zsend, zrecv, xsend, xrecv, xlocal, wsend, wrecv,
+    local_sem, info_sem, zsend, zrecv, xsend, xrecv, xlocal, xsend_alone, frecv, flocal, out_sem, wsend, wrecv,
     osend, orecv_sem, olocal, rsend, rrecv, gsend_sem, grecv_sem, usend, urecv_sem,
 ):
     y = lax.axis_index("dp")
@@ -74,6 +74,16 @@
     w_copy = pltpu.make_async_copy(w_ref, wg.at[pl.ds(y * PART, PART)], local_sem.at[1])
     w_copy.start()
 
+    ids = ids_ref[...]
+
+    def look_up(n, slot):
+        return jnp.where(ids == n, table[n], slot)
+
+    slot_of = lax.fori_loop(0, NX * NZ * NC, look_up, jnp.zeros((8, TOK), jnp.int32), unroll=4)
+    info_ref[...] = jnp.full((16, 128), -1.0, f32)
+    info_ref[0:8, :TOK] = slot_of.astype(f32)
+    info_ref[8:16, :TOK] = comb_ref[...]
+
     bar = pltpu.get_barrier_semaphore()
     for r in range(1, 8):
         for dev in (xdev(lax.rem(me + r, 8)), zdev(zat(r))):
@@ -82,19 +92,17 @@
         pl.semaphore_signal(bar, inc=1, device_id=dev, device_id_type=MESH)
     pl.semaphore_wait(bar, 16)
 
+    def send_own(t, h):
+        src = (tok_ref, cot_ref)[t]
+        for way in (0, 1):
+            rcopy(
+                src.at[:, pl.ds(h * HALF, HALF)], near.at[t, z, h],
+                zsend.at[t, way], zrecv.at[t, way, 0, h], znext[way],
+            ).start()
+
+    send_own(0, 0)
     for r in range(1, NZ):
         rcopy(info_ref, info_all.at[z], info_sem.at[0], info_sem.at[1], zdev(zat(r))).start()
-
-    def send_own(t):
-        src = (tok_ref, cot_ref)[t]
-        for h in (0, 1):
-            for way in (0, 1):
-                rcopy(
-                    src.at[:, pl.ds(h * HALF, HALF)], near.at[t, z, h],
-                    zsend.at[t, way], zrecv.at[t, way, 0, h], znext[way],
-                ).start()
-
-    send_own(0)
     for way in (0, 1):
         for h in (way, 1 - way):
             rows = pl.ds(h * (PART // 2), PART // 2)
@@ -119,7 +127,6 @@
             await_bytes(wg.at[pl.ds(base, PART // 2)], wrecv.at[way, 2])
 
     info_all[z] = info_ref[...]
-    await_bytes(info_all.at[pl.ds(0, NZ - 1)], info_sem.at[1])
     before = (
         lax.broadcasted_iota(jnp.int32, (128, 128), 0) < lax.broadcasted_iota(jnp.int32, (128, 128), 1)
     ).astype(f32)
@@ -128,6 +135,7 @@
     place = lax.broadcasted_iota(jnp.int32, (16, 128), 0)
 
     def tables(off, carry):
+        off = jnp.asarray(off, jnp.int32)
         one = info_all[lax.rem(z + off, NZ)]
         here = jnp.zeros((8, 128), f32)
         weight = jnp.zeros((8, 128), f32)
@@ -157,26 +165,48 @@
         back_lo[off] = (turned - high.astype(f32)).astype(bf16)
         return carry
 
-    lax.fori_loop(0, NZ, tables, 0)
+    tables(0, 0)
+    def pack(t, off_a, rows_a, off_b, rows_b):
+        rows = dot(pick[off_a][:, :TOK], rows_a) + dot(pick[off_b][:, :TOK], rows_b)
+        if t == 1:
+            weight = scale[off_a][:, :1]
+            rows = rows * (weight if off_a == off_b else weight + scale[off_b][:, :1])
+        return rows.astype(bf16)
+
+    def spread(src, dst, there, sems):
+        ssem, rsem, lsem = sems
+
+        def send(r, carry):
+            j = lax.rem(me + r, 8)
+            rcopy(src(j), dst(there), ssem, rsem, xdev(j)).start()
+            return carry
+
+        lax.fori_loop(1, 8, send, 0)
+        pltpu.make_async_copy(src(me), dst(there), lsem).start()
 
     def gather(t, s, h, off_a, off_b, rows_a, rows_b):
         cols = pl.ds(h * HALF, HALF)
-        rows = dot(pick[off_a][:, :TOK], rows_a) + dot(pick[off_b][:, :TOK], rows_b)
+        xs[t, s - 1, :, cols] = pack(t, off_a, rows_a, off_b, rows_b)
+        spread(
+            lambda j: xs.at[t, s - 1, pl.ds(j * 16, 16), cols], lambda at: xr.at[t, pl.ds(at, 16), cols],
+            me * 64 + s * 16, (xsend.at[t], xrecv.at[t], xlocal.at[t]),
+        )
+
+    def gather_alone(t, which, off, low, high):
+        cut = 120 if which == 0 else 8
+
+        def turn(value):
+            return jnp.concatenate([value[cut:], value[:cut]], axis=0)
+
+        rows = dot(pick[off][:, :TOK], low) + dot(turn(pick[off])[:, :TOK], high)
         if t == 1:
-            rows = rows * (scale[off_a][:, :1] + scale[off_b][:, :1])
-        xs[t, s, :, cols] = rows.astype(bf16)
-        mine = pl.ds(me * 64 + s * 16, 16)
-
-        def send(r, carry):
-            j = lax.rem(me + r, 8)
-            rcopy(
-                xs.at[t, s, pl.ds(j * 16, 16), cols], xr.at[t, mine, cols],
-                xsend.at[t], xrecv.at[t], xdev(j),
-            ).start()
-            return carry
-
-        lax.fori_loop(1, 8, send, 0)
-        pltpu.make_async_copy(xs.at[t, s, pl.ds(me * 16, 16), cols], xr.at[t, mine, cols], xlocal.at[t]).start()
+            weight = scale[off]
+            rows = rows * (weight + turn(weight))[:, :1]
+        xs_alone[t, which] = rows.astype(bf16)
+        spread(
+            lambda j: xs_alone.at[t, which, pl.ds(j * 16, 16)], lambda at: fold.at[t, which, pl.ds(at, 16)],
+            me * 16, (xsend_alone.at[t], frecv.at[t, which], flocal.at[t, which]),
+        )
 
     def step(t, s, h):
         for way in (0, 1):
@@ -186,30 +216,55 @@
                 rcopy(chunk, chunk, zsend.at[t, way], zrecv.at[t, way, s, h], znext[way]).start()
         gather(t, s, h, NZ - s, s, near[t, zat(-s), h], near[t, zat(s), h])
 
-    def last_step(t, h):
+    def own_step(t):
+        src = (tok_ref, cot_ref)[t]
+        gather_alone(t, 0, 0, src[:, :HALF], src[:, HALF:])
+
+    def far_step(t):
         far = zat(4)
-        await_bytes(near.at[t, far, h], zrecv.at[t, h, 3, h])
-        own = (tok_ref, cot_ref)[t][:, h * HALF : (h + 1) * HALF]
-        gather(t, 0, h, 0, 4, own, near[t, far, h])
-
-    for s in (1, 2, 3):
         for h in (0, 1):
-            step(0, s, h)
-        if s == 2:
-            send_own(1)
-        if s == 3:
-            weights_on()
-    for h in (0, 1):
-        last_step(0, h)
-    for s in (1, 2, 3):
-        for h in (0, 1):
-            step(1, s, h)
-    for h in (0, 1):
-        last_step(1, h)
+            await_bytes(near.at[t, far, h], zrecv.at[t, h, 3, h])
+        gather_alone(t, 1, 4, near[t, far, 0], near[t, far, 1])
+
+    send_own(0, 1)
+    own_step(0)
+    own_step(1)
+    await_bytes(info_all.at[pl.ds(0, NZ - 1)], info_sem.at[1])
+    lax.fori_loop(1, NZ, tables, 0)
+    step(0, 1, 0)
+    step(0, 1, 1)
+    send_own(1, 0)
+    send_own(1, 1)
+    step(0, 2, 0)
+    step(0, 2, 1)
+    step(1, 1, 0)
+    step(1, 1, 1)
+    weights_on()
+    step(0, 3, 0)
+    step(0, 3, 1)
+    step(1, 2, 0)
+    step(1, 2, 1)
+    far_step(0)
+    step(1, 3, 0)
+    step(1, 3, 1)
+    far_step(1)
 
     def rows_in(t):
-        await_bytes(xr.at[t, pl.ds(0, 448)], xrecv.at[t])
-        await_bytes(xr.at[t, pl.ds(0, 64)], xlocal.at[t])
+        for which in (0, 1):
+            await_bytes(fold.at[t, which, pl.ds(0, 112)], frecv.at[t, which])
+            await_bytes(fold.at[t, which, pl.ds(0, 16)], flocal.at[t, which])
+
+        def unfold(j, carry):
+            block = pl.ds(pl.multiple_of(j * 16, 16), 16)
+            own, far = fold[t, 0, block].astype(f32), fold[t, 1, block].astype(f32)
+            into = pl.ds(pl.multiple_of(j * 64, 64), 16)
+            xr[t, into, :HALF] = jnp.concatenate([own[:8], far[8:]], axis=0).astype(bf16)
+            xr[t, into, HALF:] = jnp.concatenate([own[8:], far[:8]], axis=0).astype(bf16)
+            return carry
+
+        lax.fori_loop(0, 8, unfold, 0)
+        await_bytes(xr.at[t, pl.ds(0, 336)], xrecv.at[t])
+        await_bytes(xr.at[t, pl.ds(0, 48)], xlocal.at[t])
 
     rows_in(0)
     weights_in()
@@ -236,22 +291,14 @@
 
     lax.fori_loop(0, 8, out_rows, 0)
 
-    def send_back(t):
-        for s in (0, 3, 2, 1):
-            def send(r, carry, s=s):
-                j = lax.rem(me + r, 8)
-                rcopy(
-                    orow.at[t, pl.ds(j * 64 + s * 16, 16)], orecv.at[t, s, pl.ds(me * 16, 16)],
-                    osend.at[t], orecv_sem.at[t, s], xdev(j),
-                ).start()
-                return carry
-
-            lax.fori_loop(1, 8, send, 0)
-            pltpu.make_async_copy(
-                orow.at[t, pl.ds(me * 64 + s * 16, 16)], orecv.at[t, s, pl.ds(me * 16, 16)], olocal.at[t, s]
-            ).start()
-
-    send_back(0)
+    def send_back(t, s):
+        spread(
+            lambda j: orow.at[t, pl.ds(j * 64 + s * 16, 16)], lambda at: orecv.at[t, s, pl.ds(at, 16)],
+            me * 16, (osend.at[t], orecv_sem.at[t, s], olocal.at[t, s]),
+        )
+
+    send_back(0, 0)
+    send_back(0, 3)
 
     rows_in(1)
 
@@ -285,14 +332,6 @@
             gsend_sem.at[way], grecv_sem.at[way, message], ynext[way],
         ).start()
 
-    weight_grad(2, gsend.at[0])
-    send_grad(0, 0, 0, 0)
-    send_grad(1, 0, 0, 2)
-    weight_grad(1, gsend.at[1])
-    send_grad(0, 1, 1, 2)
-    weight_grad(-1, gsend.at[2])
-    send_grad(1, 1, 2, 0)
-
     def pass_on(first):
         for way in (0, 1):
             message = 0 if first else 3
@@ -357,59 +396,72 @@
         s = (4 - k) % 4
         await_bytes(orecv.at[t, s, pl.ds(0, 112)], orecv_sem.at[t, s])
         await_bytes(orecv.at[t, s, pl.ds(0, 16)], olocal.at[t, s])
-        for way in (0, 1):
-            off = (4 - k) if way == 0 else (4 + k)
-            if k == 1:
-                await_bytes(rs_in.at[t, way, 0, way], rrecv.at[t, way, 0])
-            if k > 1:
-                await_bytes(rs_in.at[t, way, k - 1], rrecv.at[t, way, k - 1])
-            for h in (0, 1):
+        for turn in (0, 1):
+            for way in (0, 1):
+                off = (4 - k) if way == 0 else (4 + k)
+                h = way if turn == 1 else 1 - way
                 if k == 0 and h != way:
                     continue
-
-                def one(cols, inner, way=way, off=off, h=h):
+                adds = k > 1 or (k == 1 and h == way)
+                if adds:
+                    await_bytes(rs_in.at[t, way, k - 1, h], rrecv.at[t, way, k - 1, h])
+
+                def one(cols, inner):
                     total = partial(t, off, s, cols)
-                    if k > 1 or (k == 1 and h == way):
+                    if adds:
                         total = total + rs_in[t, way, k - 1, h, :, inner].astype(f32)
                     rs_out[t, way, k, h, :, inner] = total.astype(bf16)
 
                 over_tiles(h, one)
-            out, into = rs_out.at[t, way, k], rs_in.at[t, way, k]
-            if k == 0:
-                out, into = out.at[way], into.at[way]
-            rcopy(out, into, rsend.at[t, way, k], rrecv.at[t, way, k], znext[way]).start()
+                rcopy(
+                    rs_out.at[t, way, k, h], rs_in.at[t, way, k, h],
+                    rsend.at[t, way], rrecv.at[t, way, k, h], znext[way],
+                ).start()
 
     def reduce_last(t):
-        for way in (0, 1):
-            await_bytes(rs_in.at[t, way, 3], rrecv.at[t, way, 3])
         for h in (0, 1):
-            def one(cols, inner, h=h):
+            for way in (0, 1):
+                await_bytes(rs_in.at[t, way, 3, h], rrecv.at[t, way, 3, h])
+
+            def one(cols, inner):
                 total = partial(t, 0, 0, cols)
                 total = total + rs_in[t, 0, 3, h, :, inner].astype(f32) + rs_in[t, 1, 3, h, :, inner].astype(f32)
-                (lo_ref, tg_ref)[t][:, cols] = total.astype(bf16)
+                sums[t, :, cols] = total.astype(bf16)
 
             over_tiles(h, one)
-
-    reduce_step(0, 0)
+        pltpu.make_async_copy(sums.at[t], (lo_ref, tg_ref)[t], out_sem.at[t]).start()
 
     def dx_rows(n, carry):
         part = pl.ds(pl.multiple_of(n * 256, 256), 256)
         orow[1, :, part] = dot(d_pre[...], wg[part, :FF2], 1, 1).astype(bf16)
         return carry
 
+    weight_grad(2, gsend.at[0])
+    send_grad(0, 0, 0, 0)
+    send_grad(1, 0, 0, 2)
+    send_back(0, 2)
+    weight_grad(1, gsend.at[1])
+    weight_grad(-1, gsend.at[2])
+    send_grad(0, 1, 1, 2)
+    send_grad(1, 1, 2, 0)
     lax.fori_loop(0, 8, dx_rows, 0)
-    send_back(1)
+    send_back(0, 1)
+    reduce_step(0, 0)
+    send_back(1, 0)
     pass_on(True)
-    second_round()
     reduce_step(0, 1)
+    send_back(1, 3)
     weight_grad(0, gown)
     mom_copy.wait()
+    second_round()
     reduce_step(0, 2)
+    send_back(1, 2)
     reduce_step(0, 3)
+    send_back(1, 1)
     adam(True)
     reduce_step(1, 0)
+    pass_on(False)
     reduce_last(0)
-    pass_on(False)
     reduce_step(1, 1)
     reduce_step(1, 2)
     adam(False)
@@ -422,36 +474,39 @@
 
         def choose(n, carry, piece=piece):
             there = pl.ds(pl.multiple_of(piece * PIECE + n * 16, 16), 16)
-            up_ref[there] = jnp.where(swapped, urecv[there].astype(f32), uown[there].astype(f32)).astype(bf16)
+            upd[there] = jnp.where(swapped, urecv[there].astype(f32), uown[there].astype(f32)).astype(bf16)
             return carry
 
         lax.fori_loop(0, PIECE // 16, choose, 0)
-
+        rows = pl.ds(piece * PIECE, PIECE)
+        pltpu.make_async_copy(upd.at[rows], up_ref.at[rows], out_sem.at[2]).start()
+
+    for t in (0, 1):
+        await_bytes(sums.at[t], out_sem.at[t])
+    await_bytes(upd, out_sem.at[2])
     await_bytes(info_all.at[pl.ds(0, NZ - 1)], info_sem.at[0])
     await_bytes(uown, usend.at[0])
     for way in (0, 1):
         await_bytes(wg.at[pl.ds(0, PART + PART // 2)], wsend.at[way])
         await_bytes(grecv.at[way], gsend_sem.at[way])
     for t in (0, 1):
-        await_bytes(xr.at[t, pl.ds(0, 448)], xsend.at[t])
+        await_bytes(xr.at[t, pl.ds(0, 336)], xsend.at[t])
+        await_bytes(xs_alone.at[t, :, pl.ds(0, 112)], xsend_alone.at[t])
         await_bytes(orow.at[t, pl.ds(0, 448)], osend.at[t])
         for way in (0, 1):
             await_bytes(near.at[t, pl.ds(0, 7), 0], zsend.at[t, way])
-            await_bytes(rs_out.at[t, way, 0, way], rsend.at[t, way, 0])
-            for k in (1, 2, 3):
-                await_bytes(rs_out.at[t, way, k], rsend.at[t, way, k])
+            await_bytes(near.at[t, pl.ds(0, 7), 0], rsend.at[t, way])
+
+
+def hand_over(a, b, c, a_out, b_out, c_out):
+    a_out[...] = a[...]
+    b_out[...] = b[...]
+    c_out[...] = c[...]
 
 
 def local(tokens, cotangent, expert_ids, combine, slot_table, swap_flags, weights, moments):
-    experts = slot_table.shape[0]
-    slot_range = jnp.arange(experts, dtype=jnp.int32)
-    turned = expert_ids.T
-    slots = jnp.sum(
-        jnp.where(turned[:, :, None] == slot_range[None, None, :], slot_table[None, None, :], 0), axis=2
-    )
-    info = jnp.concatenate([slots.astype(f32), combine.T], axis=0)
-    info = jnp.pad(info, ((0, 0), (0, 128 - TOK)), constant_values=-1.0)
     vmem = pl.BlockSpec(memory_space=pltpu.VMEM)
+    smem = pl.BlockSpec(memory_space=pltpu.SMEM)
     anyw = pl.BlockSpec(memory_space=pl.ANY)
     dma = pltpu.SemaphoreType.DMA
     layer_out, token_grad, update = pl.pallas_call(
@@ -461,17 +516,22 @@
             jax.ShapeDtypeStruct((TOK, D), bf16),
             jax.ShapeDtypeStruct((PART, FF3), bf16),
         ),
-        in_specs=[pl.BlockSpec(memory_space=pltpu.SMEM), vmem, vmem, vmem, anyw, anyw],
-        out_specs=(vmem, vmem, vmem),
+        in_specs=[smem, smem, vmem, vmem, vmem, vmem, anyw, anyw],
+        out_specs=(anyw, anyw, anyw),
         scratch_shapes=[
+            pltpu.VMEM((16, 128), f32),
             pltpu.VMEM((NZ, 16, 128), f32),
+            pltpu.VMEM((2, TOK, D), bf16),
+            pltpu.VMEM((PART, FF3), bf16),
+            pltpu.VMEM((2, 2, 128, HALF), bf16),
             pltpu.VMEM((NZ, 128, 128), bf16),
+            pltpu.VMEM((2, 2, 128, HALF), bf16),
             pltpu.VMEM((NZ, 128, 128), bf16),
             pltpu.VMEM((NZ, 128, 128), bf16),
             pltpu.VMEM((NZ, 128, 128), bf16),
             pltpu.VMEM((NZ, 128, 128), f32),
             pltpu.VMEM((2, NZ, 2, TOK, HALF), bf16),
-            pltpu.VMEM((2, 4, 128, D), bf16),
+            pltpu.VMEM((2, 3, 128, D), bf16),
             pltpu.VMEM((2, ROWS, D), bf16),
             pltpu.VMEM((D, FF3), bf16),
             pltpu.VMEM((2, ROWS, D), bf16),
@@ -495,12 +555,16 @@
             dma((2,)),
             dma((2,)),
             dma((2,)),
+            dma((2, 2)),
+            dma((2, 2)),
+            dma((3,)),
+            dma((2,)),
             dma((2, 3)),
             dma((2,)),
             dma((2, 4)),
             dma((2, 4)),
-            dma((2, 2, 4)),
-            dma((2, 2, 4)),
+            dma((2, 2)),
+            dma((2, 2, 4, 2)),
             dma((2,)),
             dma((2, 6)),
             dma((1,)),
@@ -511,8 +575,18 @@
         ),
         cost_estimate=pl.CostEstimate(flops=8 * 10**9, bytes_accessed=9 * 10**6, transcendentals=10**6),
         name="moe_step",
-    )(swap_flags, info, tokens, cotangent, weights[0], moments[:, 0])
-    return layer_out, token_grad, update[None]
+    )(swap_flags, slot_table, expert_ids.T, combine.T, tokens, cotangent, weights[0], moments[:, 0])
+    return pl.pallas_call(
+        hand_over,
+        out_shape=(
+            jax.ShapeDtypeStruct((TOK, D), bf16),
+            jax.ShapeDtypeStruct((TOK, D), bf16),
+            jax.ShapeDtypeStruct((1, PART, FF3), bf16),
+        ),
+        in_specs=[vmem] * 3,
+        out_specs=(vmem,) * 3,
+        name="hand_over",
+    )(layer_out, token_grad, update[None])
 
 
 def solution(mesh):

time: 154 us -> 138 us (0.90)
  the two profiles are of different devices: /device:TPU:109 before, /device:TPU:1 now
where the time goes in v2:
time: 138 us
  Pallas kernels  137 us (99%)
    pallas_call x1, Pallas kernels, local(): pl.pallas_call(kernel, out_shape=(jax.ShapeDtypeStruct((TOK, D), bf16), j...  134 us

profile of v2, /device:TPU:1, one launch (start us, length us, event | category | flops | bytes accessed | tf_op | source)
XLA Modules:
  0.0 137.6 jit_solution(938098660736704738)
XLA Ops:
  0.6 134.3 %moe_step.1 = (bf16[64,2048]{1,0:T(8,128)(2,1)}, bf16[64,2048]{1,0:T(8,128)(2,1)}, bf16[512,1152]{1,0:T(8,128)(2,1)}) custom-call(s32[32]{0:T(128)} %flags.1, s32[64]{0:T(128)} %table.1, s32[8,64]{1,0:T(8,128)} %bitcast.8, f32[8,64]{1,0:T(8,128)} %bitcast.9, bf16[64,2048]{1,0:T(8,128)(2,1)} %tok_ref.1, bf16[64,2048]{1,0:T(8,128)(2,1)} %cot_ref.1, ...), custom_call_target="tpu_custom_call" | custom-call | flops 8000000000 | bytes 9000000 | tf_op jit(solution)/shard_map/moe_step/pallas_call | solution.py:512
  135.0 2.6 %hand_over.1 = (bf16[64,2048]{1,0:T(8,128)(2,1)}, bf16[64,2048]{1,0:T(8,128)(2,1)}, bf16[1,512,1152]{2,1,0:T(8,128)(2,1)}) custom-call(bf16[64,2048]{1,0:T(8,128)(2,1)} %get-tuple-element.6.a, bf16[64,2048]{1,0:T(8,128)(2,1)} %get-tuple-element.7.b, bf16[1,512,1152]{2,1,0:T(8,128)(2,1)} %bitcast.5), custom_call_target="tpu_custom_call" | custom-call | tf_op jit(solution)/shard_map/hand_over/pallas_call | solution.py:579

commit v3 on v2

--- a/solution.py
+++ b/solution.py
@@ -74,22 +74,23 @@
     w_copy = pltpu.make_async_copy(w_ref, wg.at[pl.ds(y * PART, PART)], local_sem.at[1])
     w_copy.start()
 
-    ids = ids_ref[...]
-
-    def look_up(n, slot):
-        return jnp.where(ids == n, table[n], slot)
-
-    slot_of = lax.fori_loop(0, NX * NZ * NC, look_up, jnp.zeros((8, TOK), jnp.int32), unroll=4)
-    info_ref[...] = jnp.full((16, 128), -1.0, f32)
-    info_ref[0:8, :TOK] = slot_of.astype(f32)
-    info_ref[8:16, :TOK] = comb_ref[...]
-
     bar = pltpu.get_barrier_semaphore()
     for r in range(1, 8):
         for dev in (xdev(lax.rem(me + r, 8)), zdev(zat(r))):
             pl.semaphore_signal(bar, inc=1, device_id=dev, device_id_type=MESH)
     for dev in ynext:
         pl.semaphore_signal(bar, inc=1, device_id=dev, device_id_type=MESH)
+
+    ids = ids_ref[...]
+
+    def look_up(n, slot):
+        return jnp.where(ids == n, table[n], slot)
+
+    slot_of = lax.fori_loop(0, NX * NZ * NC, look_up, jnp.zeros((8, TOK), jnp.int32), unroll=4)
+    info_ref[...] = jnp.full((16, 128), -1.0, f32)
+    info_ref[0:8, :TOK] = slot_of.astype(f32)
+    info_ref[8:16, :TOK] = comb_ref[...]
+
     pl.semaphore_wait(bar, 16)
 
     def send_own(t, h):
@@ -103,13 +104,16 @@
     send_own(0, 0)
     for r in range(1, NZ):
         rcopy(info_ref, info_all.at[z], info_sem.at[0], info_sem.at[1], zdev(zat(r))).start()
-    for way in (0, 1):
-        for h in (way, 1 - way):
+    def send_weights(first):
+        for way in (0, 1):
+            h = way if first else 1 - way
             rows = pl.ds(h * (PART // 2), PART // 2)
             rcopy(
                 w_ref.at[rows], wg.at[pl.ds(y * PART + h * (PART // 2), PART // 2)],
                 wsend.at[way], wrecv.at[way, h], ynext[way],
             ).start()
+
+    send_weights(True)
 
     def weights_on():
         for way in (0, 1):
@@ -208,12 +212,14 @@
             me * 16, (xsend_alone.at[t], frecv.at[t, which], flocal.at[t, which]),
         )
 
-    def step(t, s, h):
+    def pass_chunks(t, s, h):
         for way in (0, 1):
             chunk = near.at[t, zat(-s if way == 0 else s), h]
             await_bytes(chunk, zrecv.at[t, way, s - 1, h])
             if s < 3 or h == way:
                 rcopy(chunk, chunk, zsend.at[t, way], zrecv.at[t, way, s, h], znext[way]).start()
+
+    def collect(t, s, h):
         gather(t, s, h, NZ - s, s, near[t, zat(-s), h], near[t, zat(s), h])
 
     def own_step(t):
@@ -225,29 +231,6 @@
         for h in (0, 1):
             await_bytes(near.at[t, far, h], zrecv.at[t, h, 3, h])
         gather_alone(t, 1, 4, near[t, far, 0], near[t, far, 1])
-
-    send_own(0, 1)
-    own_step(0)
-    own_step(1)
-    await_bytes(info_all.at[pl.ds(0, NZ - 1)], info_sem.at[1])
-    lax.fori_loop(1, NZ, tables, 0)
-    step(0, 1, 0)
-    step(0, 1, 1)
-    send_own(1, 0)
-    send_own(1, 1)
-    step(0, 2, 0)
-    step(0, 2, 1)
-    step(1, 1, 0)
-    step(1, 1, 1)
-    weights_on()
-    step(0, 3, 0)
-    step(0, 3, 1)
-    step(1, 2, 0)
-    step(1, 2, 1)
-    far_step(0)
-    step(1, 3, 0)
-    step(1, 3, 1)
-    far_step(1)
 
     def rows_in(t):
         for which in (0, 1):
@@ -266,30 +249,31 @@
         await_bytes(xr.at[t, pl.ds(0, 336)], xrecv.at[t])
         await_bytes(xr.at[t, pl.ds(0, 48)], xlocal.at[t])
 
-    rows_in(0)
-    weights_in()
-
-    def project(n, carry):
-        cols = pl.ds(pl.multiple_of(n * 256, 256), 256)
-        proj[:, cols] = dot(xr[0], wg[:, cols])
-        return carry
-
-    lax.fori_loop(0, 3, project, 0)
-
-    def activate(n, carry):
-        rows = pl.ds(pl.multiple_of(n * 64, 64), 64)
-        gate = proj[rows, :FF]
-        hidden[rows] = (gate * jax.nn.sigmoid(gate) * proj[rows, FF:]).astype(bf16)
-        return carry
-
-    lax.fori_loop(0, 8, activate, 0)
-
-    def out_rows(n, carry):
-        part = pl.ds(pl.multiple_of(n * 256, 256), 256)
-        orow[0, :, part] = dot(hidden[...], wg[part, FF2:], 1, 1).astype(bf16)
-        return carry
-
-    lax.fori_loop(0, 8, out_rows, 0)
+    def forward():
+        rows_in(0)
+        weights_in()
+
+        def project(n, carry):
+            cols = pl.ds(pl.multiple_of(n * 256, 256), 256)
+            proj[:, cols] = dot(xr[0], wg[:, cols])
+            return carry
+
+        lax.fori_loop(0, 3, project, 0)
+
+        def activate(n, carry):
+            rows = pl.ds(pl.multiple_of(n * 64, 64), 64)
+            gate = proj[rows, :FF]
+            hidden[rows] = (gate * jax.nn.sigmoid(gate) * proj[rows, FF:]).astype(bf16)
+            return carry
+
+        lax.fori_loop(0, 8, activate, 0)
+
+        def out_rows(n, carry):
+            part = pl.ds(pl.multiple_of(n * 256, 256), 256)
+            orow[0, :, part] = dot(hidden[...], wg[part, FF2:], 1, 1).astype(bf16)
+            return carry
+
+        lax.fori_loop(0, 8, out_rows, 0)
 
     def send_back(t, s):
         spread(
@@ -297,6 +281,42 @@
             me * 16, (osend.at[t], orecv_sem.at[t, s], olocal.at[t, s]),
         )
 
+    send_own(0, 1)
+    own_step(0)
+    own_step(1)
+    await_bytes(info_all.at[pl.ds(0, NZ - 1)], info_sem.at[1])
+    lax.fori_loop(1, NZ, tables, 0)
+    pass_chunks(0, 1, 0)
+    collect(0, 1, 0)
+    pass_chunks(0, 1, 1)
+    collect(0, 1, 1)
+    send_weights(False)
+    send_own(1, 0)
+    send_own(1, 1)
+    pass_chunks(0, 2, 0)
+    collect(0, 2, 0)
+    pass_chunks(0, 2, 1)
+    collect(0, 2, 1)
+    weights_on()
+    pass_chunks(1, 1, 0)
+    collect(1, 1, 0)
+    pass_chunks(1, 1, 1)
+    collect(1, 1, 1)
+    pass_chunks(0, 3, 0)
+    collect(0, 3, 0)
+    pass_chunks(0, 3, 1)
+    collect(0, 3, 1)
+    pass_chunks(1, 2, 0)
+    collect(1, 2, 0)
+    pass_chunks(1, 2, 1)
+    collect(1, 2, 1)
+    far_step(0)
+    pass_chunks(1, 3, 0)
+    collect(1, 3, 0)
+    pass_chunks(1, 3, 1)
+    collect(1, 3, 1)
+    far_step(1)
+    forward()
     send_back(0, 0)
     send_back(0, 3)
 
@@ -440,11 +460,11 @@
     send_grad(0, 0, 0, 0)
     send_grad(1, 0, 0, 2)
     send_back(0, 2)
+    lax.fori_loop(0, 8, dx_rows, 0)
     weight_grad(1, gsend.at[1])
     weight_grad(-1, gsend.at[2])
     send_grad(0, 1, 1, 2)
     send_grad(1, 1, 2, 0)
-    lax.fori_loop(0, 8, dx_rows, 0)
     send_back(0, 1)
     reduce_step(0, 0)
     send_back(1, 0)
@@ -453,14 +473,14 @@
     send_back(1, 3)
     weight_grad(0, gown)
     mom_copy.wait()
+    reduce_step(0, 2)
     second_round()
-    reduce_step(0, 2)
     send_back(1, 2)
     reduce_step(0, 3)
     send_back(1, 1)
     adam(True)
+    pass_on(False)
     reduce_step(1, 0)
-    pass_on(False)
     reduce_last(0)
     reduce_step(1, 1)
     reduce_step(1, 2)
@@ -498,10 +518,18 @@
             await_bytes(near.at[t, pl.ds(0, 7), 0], rsend.at[t, way])
 
 
-def hand_over(a, b, c, a_out, b_out, c_out):
-    a_out[...] = a[...]
-    b_out[...] = b[...]
-    c_out[...] = c[...]
+def hand_over(a, b, c, a_out, b_out, c_out, a_mid, b_mid, c_mid, in_sem, out_sem):
+    parts = [(c.at[0, pl.ds(n * PIECE, PIECE)], c_mid.at[pl.ds(n * PIECE, PIECE)], c_out.at[0, pl.ds(n * PIECE, PIECE)])
+             for n in range(4)] + [(a, a_mid, a_out), (b, b_mid, b_out)]
+    first = [pltpu.make_async_copy(src, mid, in_sem.at[n]) for n, (src, mid, _) in enumerate(parts)]
+    second = [pltpu.make_async_copy(mid, dst, out_sem.at[n]) for n, (_, mid, dst) in enumerate(parts)]
+    for copy in first:
+        copy.start()
+    for n, copy in enumerate(first):
+        copy.wait()
+        second[n].start()
+    for copy in second:
+        copy.wait()
 
 
 def local(tokens, cotangent, expert_ids, combine, slot_table, swap_flags, weights, moments):
@@ -583,8 +611,15 @@
             jax.ShapeDtypeStruct((TOK, D), bf16),
             jax.ShapeDtypeStruct((1, PART, FF3), bf16),
         ),
-        in_specs=[vmem] * 3,
-        out_specs=(vmem,) * 3,
+        in_specs=[anyw] * 3,
+        out_specs=(anyw,) * 3,
+        scratch_shapes=[
+            pltpu.VMEM((TOK, D), bf16),
+            pltpu.VMEM((TOK, D), bf16),
+            pltpu.VMEM((PART, FF3), bf16),
+            dma((6,)),
+            dma((6,)),
+        ],
         name="hand_over",
     )(layer_out, token_grad, update[None])
 

time: 138 us -> 137 us (level)
  no operation moved by 1% of the time
where the time goes in v3:
time: 137 us
  Pallas kernels  136 us (99%)
    pallas_call x1, Pallas kernels, local(): pl.pallas_call(kernel, out_shape=(jax.ShapeDtypeStruct((TOK, D), bf16), j...  134 us

profile of v3, /device:TPU:1, one launch (start us, length us, event | category | flops | bytes accessed | tf_op | source)
XLA Modules:
  0.0 137.1 jit_solution(12065359787887065978)
XLA Ops:
  0.6 134.2 %moe_step.1 = (bf16[64,2048]{1,0:T(8,128)(2,1)}, bf16[64,2048]{1,0:T(8,128)(2,1)}, bf16[512,1152]{1,0:T(8,128)(2,1)}) custom-call(s32[32]{0:T(128)} %flags.1, s32[64]{0:T(128)} %table.1, s32[8,64]{1,0:T(8,128)} %bitcast.8, f32[8,64]{1,0:T(8,128)} %bitcast.9, bf16[64,2048]{1,0:T(8,128)(2,1)} %tok_ref.1, bf16[64,2048]{1,0:T(8,128)(2,1)} %cot_ref.1, ...), custom_call_target="tpu_custom_call" | custom-call | flops 8000000000 | bytes 9000000 | tf_op jit(solution)/shard_map/moe_step/pallas_call | solution.py:540
  134.8 2.2 %hand_over.1 = (bf16[64,2048]{1,0:T(8,128)(2,1)}, bf16[64,2048]{1,0:T(8,128)(2,1)}, bf16[1,512,1152]{2,1,0:T(8,128)(2,1)}) custom-call(bf16[64,2048]{1,0:T(8,128)(2,1)} %get-tuple-element.6.a, bf16[64,2048]{1,0:T(8,128)(2,1)} %get-tuple-element.7.b, bf16[1,512,1152]{2,1,0:T(8,128)(2,1)} %bitcast.5), custom_call_target="tpu_custom_call" | custom-call | tf_op jit(solution)/shard_map/hand_over/pallas_call | solution.py:607
